TPU v7x, 32 devices: a whole 2x2x4 slice. The times are simulated.
32 devices in a mesh: shift: 4 (over y, x), space: 8 (over z, core).
Axes of the slice: x: 2, y: 2, z: 4, core: 2. Of those that a mesh axis runs over, the one named last changes fastest.
Arguments:
- residual: float32 [4, 128, 128, 128], P('shift', 'space'), may hold values from -6 to 6
- log_base: bfloat16 [128, 128, 128], P('space'), may hold values from -3 to 3
- mask: int32 [16, 16, 16], replicated, may hold values from 0 to 1
- gen_vector: int32 [64], replicated, may hold values from 1 to 1023
- point_index: int32 [4], P('shift'), may hold values from 0 to 1023
- shift_values: float32 [4, 64], P('shift'), may hold values from 0 to 1
Outputs:
- correction: float32 [4, 128, 128, 128], P('shift', 'space')
- mean_field: float32 [128, 128, 128], P('space', 'shift')
- square_field: float32 [128, 128, 128], P('space', 'shift')
All inputs are finite; a program needn't handle non-finite values.
Results may differ from a plain program's by a relative error of at most 0.0003.
Values sent between devices are 32-bit elements; how exact they have to be, the bound alone decides.
A program may use at most 192 MiB of HBM per device.

v0:
```python
import math

import jax
import jax.numpy as jnp
from jax import lax
from jax.sharding import PartitionSpec as P

NPTS = 1024
SWEEPS_LOW = 8


RELAX = 0.8


def with_halo(value, sides, width):
    for axis, dim in sides:
        size, length = (lax.axis_size(axis), value.shape[dim])
        up = [(i, (i + 1) % size) for i in range(size - 1)]
        down = [(j, i) for i, j in up]
        last = lax.slice_in_dim(value, length - width, length, axis=dim)
        initial = lax.slice_in_dim(value, 0, width, axis=dim)
        before = lax.ppermute(last, axis, up)
        after = lax.ppermute(initial, axis, down)
        value = jnp.concatenate([before, value, after], axis=dim)
    return value


def mode_tables(modes):
    order = jnp.arange(modes, dtype=jnp.int32)
    along_x = (order % 4 + 1).astype(jnp.float32)
    along_y = (order // 4 % 4 + 1).astype(jnp.float32)
    along_z = (order // 16 + 1).astype(jnp.float32)
    amplitude = 1.5 / jnp.sqrt(along_x * along_x + along_y * along_y + along_z * along_z)
    return (along_x, along_y, along_z, amplitude)


def cosine_table(frequency, cells, start, total):
    position = (jnp.arange(cells, dtype=jnp.int32) + start).astype(jnp.float32) + 0.5
    return jnp.cos(math.pi * frequency[:, None] * position[None, :] / total)


def lattice_sample(point, generator, offset):
    lattice = point * generator % NPTS
    shifted = lattice.astype(jnp.float32) / NPTS + offset
    fraction = shifted - jnp.floor(shifted)
    return 1.0 - 2.0 * jnp.abs(2.0 * fraction - 1.0)


def smooth_log(sample, table_x, table_y, table_z, amplitude):
    weights = (amplitude * sample)[:, None] * table_x
    outer = weights[:, :, None] * table_y[:, None, :]
    modes, rows, cols = outer.shape
    flat = outer.reshape(modes, rows * cols)
    product = lax.dot_general(
        flat,
        table_z,
        (((0,), (0,)), ((), ())),
        precision=lax.Precision.HIGHEST,
        preferred_element_type=jnp.float32,
    )
    return product.reshape(rows, cols, table_z.shape[1])


def face_weights(conduct_wide):
    center = conduct_wide[1:-1]
    padded = jnp.pad(center, ((0, 0), (1, 1), (1, 1)), mode="edge")
    face_west = 0.5 * (center + conduct_wide[:-2])
    face_east = 0.5 * (center + conduct_wide[2:])
    face_south = 0.5 * (center + padded[:, :-2, 1:-1])
    face_north = 0.5 * (center + padded[:, 2:, 1:-1])
    face_below = 0.5 * (center + padded[:, 1:-1, :-2])
    face_above = 0.5 * (center + padded[:, 1:-1, 2:])
    diagonal = face_west + face_east + face_south + face_north + face_below + face_above
    return (face_west, face_east, face_south, face_north, face_below, face_above, diagonal)


def apply_weights(faces, field_wide):
    face_west, face_east, face_south, face_north, face_below, face_above, diagonal = faces
    inner = field_wide[1:-1]
    zeroed = jnp.pad(inner, ((0, 0), (1, 1), (1, 1)))
    beside = face_west * field_wide[:-2] + face_east * field_wide[2:]
    beside = beside + face_south * zeroed[:, :-2, 1:-1] + face_north * zeroed[:, 2:, 1:-1]
    beside = beside + face_below * zeroed[:, 1:-1, :-2] + face_above * zeroed[:, 1:-1, 2:]
    return diagonal * inner - beside


def expand_blocks(blocks, size):
    rows, cols, depth = blocks.shape
    grown = jnp.broadcast_to(
        blocks[:, None, :, None, :, None], (rows, size, cols, size, depth, size)
    )
    return grown.reshape(rows * size, cols * size, depth * size)


def coarsen(values):
    rows, cols, depth = values.shape
    return values.reshape(rows // 2, 2, cols // 2, 2, depth // 2, 2).sum(axis=(1, 3, 5))


def refine(values):
    rows, cols, depth = values.shape
    grown = jnp.broadcast_to(values[:, None, :, None, :, None], (rows, 2, cols, 2, depth, 2))
    return grown.reshape(rows * 2, cols * 2, depth * 2)


def first_sweep(source, faces, active):
    return active * (RELAX * source / faces[6])


def more_sweeps(solution, source, faces, active, sweeps, widen):
    for repeat in range(sweeps):
        applied = apply_weights(faces, widen(solution))
        solution = active * (solution + RELAX * (source - applied) / faces[6])
    return solution


def defect(solution, source, faces, active, widen):
    applied = apply_weights(faces, widen(solution))
    return active * (source - applied)


def rim_top(field):
    return with_halo(field, (("space", 0),), 1)


def rim_mid(field):
    return with_halo(field, (("space", 0),), 1)


def rim_low(field):
    return with_halo(field, (("space", 0),), 1)


def local(residual, log_base, mask, gen_vector, point_index, shift_values):
    planes = residual.shape[1]
    width = residual.shape[2]
    devices = lax.axis_size("space")
    place = lax.axis_index("space")
    along_x, along_y, along_z, amplitude = mode_tables(gen_vector.shape[0])
    table_x = cosine_table(along_x, planes, place * planes, planes * devices)
    table_y = cosine_table(along_y, width, 0, width)
    table_z = cosine_table(along_z, width, 0, width)
    sample = lattice_sample(point_index[0], gen_vector, shift_values[0])
    conduct_top = jnp.exp(
        log_base.astype(jnp.float32) + smooth_log(sample, table_x, table_y, table_z, amplitude)
    )
    blocks = lax.dynamic_slice_in_dim(mask, place * (planes // 8), planes // 8, 0).astype(
        jnp.float32
    )
    first_device = place == 0
    last_device = place == devices - 1

    def bounded(conduct, rimmed):
        lower = jnp.where(first_device, conduct[0], rimmed[0])
        upper = jnp.where(last_device, conduct[-1], rimmed[-1])
        return jnp.concatenate([lower[None], conduct, upper[None]], axis=0)

    source_top = residual[0]
    active_top = expand_blocks(blocks, 8)
    faces_top = face_weights(bounded(conduct_top, rim_top(conduct_top)))
    solution_top = more_sweeps(
        first_sweep(source_top, faces_top, active_top),
        source_top,
        faces_top,
        active_top,
        1,
        rim_top,
    )
    source_mid = 0.5 * coarsen(defect(solution_top, source_top, faces_top, active_top, rim_top))
    conduct_mid = 0.125 * coarsen(conduct_top)
    active_mid = expand_blocks(blocks, 4)
    faces_mid = face_weights(bounded(conduct_mid, rim_mid(conduct_mid)))
    solution_mid = more_sweeps(
        first_sweep(source_mid, faces_mid, active_mid),
        source_mid,
        faces_mid,
        active_mid,
        1,
        rim_mid,
    )
    source_low = 0.5 * coarsen(defect(solution_mid, source_mid, faces_mid, active_mid, rim_mid))
    conduct_low = 0.125 * coarsen(conduct_mid)
    active_low = expand_blocks(blocks, 2)
    faces_low = face_weights(bounded(conduct_low, rim_low(conduct_low)))
    solution_low = more_sweeps(
        first_sweep(source_low, faces_low, active_low),
        source_low,
        faces_low,
        active_low,
        SWEEPS_LOW - 1,
        rim_low,
    )
    solution_mid = more_sweeps(
        solution_mid + refine(solution_low), source_mid, faces_mid, active_mid, 2, rim_mid
    )
    solution_top = more_sweeps(
        solution_top + refine(solution_mid), source_top, faces_top, active_top, 2, rim_top
    )
    shifts_count = lax.axis_size("shift")
    total, squares = (
        lax.psum_scatter(solution_top, "shift", scatter_dimension=1, tiled=True),
        lax.psum_scatter(solution_top * solution_top, "shift", scatter_dimension=1, tiled=True),
    )
    return (solution_top[None], total / shifts_count, squares / shifts_count)


def solution(mesh):
    placed = (
        P("shift", "space", None, None),
        P("space", None, None),
        P(),
        P(),
        P("shift"),
        P("shift", None),
    )
    return jax.shard_map(
        local,
        mesh=mesh,
        in_specs=placed,
        out_specs=(
            P("shift", "space", None, None),
            P("space", "shift", None),
            P("space", "shift", None),
        ),
        check_vma=False,
    )
```

profile of v0, /device:TPU:0, one launch (start us, length us, event | category | flops | bytes accessed | tf_op | source)
XLA Modules:
  0.0 559.9 jit_solution(12497702443127541066)
XLA Ops:
  17.1 68.4 %reshape.183 = f32[8,2,64,2,64,2]{5,4,3,2,1,0:T(8,128)} reshape(f32[16,128,128]{2,1,0:T(8,128)S(1)} %fusion) | data formatting | bytes 2097152 | tf_op jit(solution)/shard_map/reshape | solution.py:97
  85.5 20.8 %reduce_sum.37 = f32[8,64,64]{2,1,0:T(8,128)S(1)} reduce(f32[8,2,64,2,64,2]{5,4,3,2,1,0:T(8,128)} %reshape.183, f32[]{:T(128)} %constant.116.clone.1), dimensions={1,3,5}, to_apply=%region_1.2 | reduce | flops 229376 | bytes 1179652 | tf_op jit(solution)/shard_map/reduce_sum | solution.py:97
  107.0 4.6 collective-permute-start.6
  112.9 10.1 %mul.713 = f32[4,2,32,2,32,2]{5,4,3,2,1,0:T(8,128)} reshape(f32[8,64,64]{2,1,0:T(8,128)S(1)} %broadcast_multiply_fusion.3) | data formatting | bytes 262144 | tf_op jit(solution)/shard_map/mul | solution.py:170
  123.0 4.1 reduce_sum.39
  127.7 4.9 collective-permute-start.12
  136.1 7.3 %broadcast_in_dim.12 = f32[2,8,16,8,16,8]{5,4,3,2,1,0:T(8,128)} broadcast(f32[2,16,16]{2,1,0:T(8,128)S(1)} %dynamic-slice_convert_fusion), dimensions={0,2,4} | broadcast | bytes 1050624 | tf_op jit(solution)/shard_map/broadcast_in_dim | solution.py:89
  143.4 11.8 %reshape.180 = f32[16,128,128]{2,1,0:T(8,128)S(1)} reshape(f32[2,8,16,8,16,8]{5,4,3,2,1,0:T(8,128)} %broadcast_in_dim.12) | data formatting | bytes 2097152 | tf_op jit(solution)/shard_map/reshape | solution.py:92
  157.6 4.4 reshape.181
  174.7 4.4 collective-permute-start.4
  185.7 69.2 %reshape.182 = f32[8,2,64,2,64,2]{5,4,3,2,1,0:T(8,128)} reshape(f32[16,128,128]{2,1,0:T(8,128)} %fusion.22) | data formatting | bytes 2097152 | tf_op jit(solution)/shard_map/reshape | solution.py:97
  254.9 21.5 %reduce_sum.36 = f32[8,64,64]{2,1,0:T(8,128)} reduce(f32[8,2,64,2,64,2]{5,4,3,2,1,0:T(8,128)} %reshape.182, f32[]{:T(128)} %constant.116.clone.1), dimensions={1,3,5}, to_apply=%region_0.1 | reduce | flops 229376 | bytes 1179652 | tf_op jit(solution)/shard_map/reduce_sum | solution.py:97
  280.1 5.4 collective-permute-start.8
  301.1 10.9 %reshape.185 = f32[4,2,32,2,32,2]{5,4,3,2,1,0:T(8,128)} reshape(f32[8,64,64]{2,1,0:T(8,128)} %fusion.103) | data formatting | bytes 262144 | tf_op jit(solution)/shard_map/reshape | solution.py:97
  312.0 4.1 reduce_sum.38
  317.2 4.5 collective-permute-start.14
  372.6 8.8 %reshape.186 = f32[8,64,64]{2,1,0:T(8,128)} reshape(f32[4,2,32,2,32,2]{5,4,3,2,1,0:T(8,128)} %broadcast_in_dim.15) | data formatting | bytes 262144 | tf_op jit(solution)/shard_map/reshape | solution.py:103
  391.4 4.1 collective-permute-start.30
  399.0 21.5 %broadcast_in_dim.16 = f32[8,2,64,2,64,2]{5,4,3,2,1,0:T(8,128)} broadcast(f32[8,64,64]{2,1,0:T(8,128)S(1)} %fusion.131), dimensions={0,2,4} | broadcast | bytes 1179648 | tf_op jit(solution)/shard_map/broadcast_in_dim | solution.py:102
  420.5 47.1 %reshape.187 = f32[16,128,128]{2,1,0:T(8,128)} reshape(f32[8,2,64,2,64,2]{5,4,3,2,1,0:T(8,128)} %broadcast_in_dim.16) | data formatting | bytes 2097152 | tf_op jit(solution)/shard_map/reshape | solution.py:103
  469.5 4.1 collective-permute-start.32
  479.0 4.4 collective-permute-start.34
  490.5 29.5 %reduce-scatter.5.cloned.1.call-done = f32[16,32,128]{2,1,0:T(8,128)} async-done(((f32[16,128,128]{2,1,0:T(8,128)}), f32[16,32,128]{2,1,0:T(8,128)}) %reduce-scatter.5.cloned.1.call-update) | async-done | bytes 262160 | tf_op jit(solution)/shard_map/reduce_scatter | solution.py:202
  521.6 29.8 %reduce-scatter.3.cloned.1.call-done = f32[16,32,128]{2,1,0:T(8,128)} async-done(((f32[16,128,128]{2,1,0:T(8,128)}), f32[16,32,128]{2,1,0:T(8,128)}) %reduce-scatter.3.cloned.1.call-update) | async-done | bytes 262160 | tf_op jit(solution)/shard_map/reduce_scatter | solution.py:201
  (229 shorter events, 138.7 us)
Async XLA Ops:
  7.2 512.7 %reduce-scatter.5.cloned.1.call-start = ((), (), s32[]{:S(2)}) async-start(), calls=%async_computation.3 | async-start | bytes 1310720 | tf_op jit(solution)/shard_map/reduce_scatter | solution.py:202
  12.9 149.1 %collective-permute-start = (f32[1,128,128]{2,1,0:T(8,128)}, f32[1,128,128]{2,1,0:T(8,128)}, u32[]{:S(2)}, u32[]{:S(2)}) collective-permute-start(f32[1,128,128]{2,1,0:T(8,128)} %get-tuple-element.27), channel_id=1, source_target_pairs={{0,1},{1,2},{2,3},{3,4},{4,5},{5,6},{6,7},{8,9},{9,10},{10,11},{11... | collective-permute-start | bytes 196616 | tf_op jit(solution)/shard_map/ppermute | solution.py:22
  15.8 146.2 %collective-permute-start.1 = (f32[1,128,128]{2,1,0:T(8,128)}, f32[1,128,128]{2,1,0:T(8,128)}, u32[]{:S(2)}, u32[]{:S(2)}) collective-permute-start(f32[1,128,128]{2,1,0:T(8,128)} %get-tuple-element.26), channel_id=1, source_target_pairs={{1,0},{2,1},{3,2},{4,3},{5,4},{6,5},{7,6},{9,8},{10,9},{11,10},{12... | collective-permute-start | bytes 196616 | tf_op jit(solution)/shard_map/ppermute | solution.py:23
  107.0 72.1 %collective-permute-start.6 = (f32[1,64,64]{2,1,0:T(8,128)}, f32[1,64,64]{2,1,0:T(8,128)S(1)}, u32[]{:S(2)}, u32[]{:S(2)}) collective-permute-start(f32[1,64,64]{2,1,0:T(8,128)} %get-tuple-element.43), channel_id=1, source_target_pairs={{0,1},{1,2},{2,3},{3,4},{4,5},{5,6},{6,7},{8,9},{9,10},{10,11},{11... | collective-permute-start | bytes 49160 | tf_op jit(solution)/shard_map/ppermute | solution.py:22
  111.6 68.8 %collective-permute-start.7 = (f32[1,64,64]{2,1,0:T(8,128)}, f32[1,64,64]{2,1,0:T(8,128)}, u32[]{:S(2)}, u32[]{:S(2)}) collective-permute-start(f32[1,64,64]{2,1,0:T(8,128)} %get-tuple-element.42), channel_id=1, source_target_pairs={{1,0},{2,1},{3,2},{4,3},{5,4},{6,5},{7,6},{9,8},{10,9},{11,10},{12... | collective-permute-start | bytes 49160 | tf_op jit(solution)/shard_map/ppermute | solution.py:23
  127.7 170.2 %collective-permute-start.12 = (f32[1,32,32]{2,1,0:T(8,128)}, f32[1,32,32]{2,1,0:T(8,128)}, u32[]{:S(2)}, u32[]{:S(2)}) collective-permute-start(f32[1,32,32]{2,1,0:T(8,128)} %get-tuple-element.65), channel_id=1, source_target_pairs={{0,1},{1,2},{2,3},{3,4},{4,5},{5,6},{6,7},{8,9},{9,10},{10,11},{11... | collective-permute-start | bytes 12296 | tf_op jit(solution)/shard_map/ppermute | solution.py:22
  166.0 5.1 collective-permute-start.2
  171.1 126.8 %collective-permute-start.13 = (f32[1,32,32]{2,1,0:T(8,128)}, f32[1,32,32]{2,1,0:T(8,128)}, u32[]{:S(2)}, u32[]{:S(2)}) collective-permute-start(f32[1,32,32]{2,1,0:T(8,128)} %get-tuple-element.64), channel_id=1, source_target_pairs={{1,0},{2,1},{3,2},{4,3},{5,4},{6,5},{7,6},{9,8},{10,9},{11,10},{12... | collective-permute-start | bytes 12296 | tf_op jit(solution)/shard_map/ppermute | solution.py:23
  174.7 6.5 %collective-permute-start.4 = (f32[1,128,128]{2,1,0:T(8,128)S(1)}, f32[1,128,128]{2,1,0:T(8,128)S(1)}, u32[]{:S(2)}, u32[]{:S(2)}) collective-permute-start(f32[1,128,128]{2,1,0:T(8,128)S(1)} %get-tuple-element.20), channel_id=1, source_target_pairs={{0,1},{1,2},{2,3},{3,4},{4,5},{5,6},{6,7},{8,9},{9,10},{10,11},{11... | collective-permute-start | bytes 196616 | tf_op jit(solution)/shard_map/ppermute | solution.py:22
  280.1 10.9 %collective-permute-start.8 = (f32[1,64,64]{2,1,0:T(8,128)}, f32[1,64,64]{2,1,0:T(8,128)}, u32[]{:S(2)}, u32[]{:S(2)}) collective-permute-start(f32[1,64,64]{2,1,0:T(8,128)} %get-tuple-element.38), channel_id=1, source_target_pairs={{0,1},{1,2},{2,3},{3,4},{4,5},{5,6},{6,7},{8,9},{9,10},{10,11},{11... | collective-permute-start | bytes 49160 | tf_op jit(solution)/shard_map/ppermute | solution.py:22
  285.5 5.4 collective-permute-start.9
  293.6 5.7 %collective-permute-start.10 = (f32[1,64,64]{2,1,0:T(8,128)S(1)}, f32[1,64,64]{2,1,0:T(8,128)S(1)}, u32[]{:S(2)}, u32[]{:S(2)}) collective-permute-start(f32[1,64,64]{2,1,0:T(8,128)S(1)} %get-tuple-element.36), channel_id=1, source_target_pairs={{0,1},{1,2},{2,3},{3,4},{4,5},{5,6},{6,7},{8,9},{9,10},{10,11},{11... | collective-permute-start | bytes 49160 | tf_op jit(solution)/shard_map/ppermute | solution.py:22
  317.2 5.8 %collective-permute-start.14 = (f32[1,32,32]{2,1,0:T(8,128)S(1)}, f32[1,32,32]{2,1,0:T(8,128)S(1)}, u32[]{:S(2)}, u32[]{:S(2)}) collective-permute-start(f32[1,32,32]{2,1,0:T(8,128)S(1)} %get-tuple-element.60), channel_id=1, source_target_pairs={{0,1},{1,2},{2,3},{3,4},{4,5},{5,6},{6,7},{8,9},{9,10},{10,11},{11... | collective-permute-start | bytes 12296 | tf_op jit(solution)/shard_map/ppermute | solution.py:22
  325.8 5.2 collective-permute-start.16
  333.0 5.2 collective-permute-start.18
  340.1 5.2 collective-permute-start.20
  347.2 5.2 collective-permute-start.22
  354.4 5.2 collective-permute-start.24
  361.5 5.4 collective-permute-start.26
  382.5 5.4 collective-permute-start.28
  391.4 5.4 collective-permute-start.30
  469.5 5.4 collective-permute-start.32
  479.0 5.7 %collective-permute-start.34 = (f32[1,128,128]{2,1,0:T(8,128)S(1)}, f32[1,128,128]{2,1,0:T(8,128)S(1)}, u32[]{:S(2)}, u32[]{:S(2)}) collective-permute-start(f32[1,128,128]{2,1,0:T(8,128)S(1)} %get-tuple-element.16), channel_id=1, source_target_pairs={{0,1},{1,2},{2,3},{3,4},{4,5},{5,6},{6,7},{8,9},{9,10},{10,11},{11... | collective-permute-start | bytes 196616 | tf_op jit(solution)/shard_map/ppermute | solution.py:22
  489.7 61.7 %reduce-scatter.3.cloned.1.call-start = ((), (), s32[]{:S(2)}) async-start(), calls=%async_computation.2 | async-start | bytes 1310720 | tf_op jit(solution)/shard_map/reduce_scatter | solution.py:201
  (60 other events, 948.4 us)
Sparse Core Ops, SparseCore 0:
  489.8 30.0 reduce-scatter.4
  523.6 27.7 reduce-scatter.2
where the time goes:
time: 563 us; the launch traced here: 560 us
  local copies, waits for them, and re-layouts  276 us (49%)
  starting transfers between devices  96.4 us (17%)
  other arithmetic  87 us (15%)
  waiting for transfers between devices  81.6 us (14%)
  between operations  15.9 us (3%)
    reshape x3, local copies, waits for them, and re-layouts, coarsen(): values.reshape(rows // 2, 2, cols // 2, 2, depth // 2, 2)  148 us
    ppermute x18, starting transfers between devices, with_halo(): before = lax.ppermute(last, axis, up)  72.9 us
    reshape x2, local copies, waits for them, and re-layouts, refine(): return grown.reshape(rows * 2, cols * 2, depth * 2)  55.9 us
    reduce_sum x4, other arithmetic, coarsen(): values.reshape(rows // 2, 2, cols // 2, 2, depth // 2, 2)  50.4 us
    reduce_scatter x1, waiting for transfers between devices, local(): lax.psum_scatter(solution_top, 'shift', scatter_dimension=1, tiled=True)  29.8 us
    reduce_scatter x1, waiting for transfers between devices, local(): lax.psum_scatter(solution_top * solution_top, 'shift', scatter_dimension=...  29.5 us
    broadcast_in_dim x2, local copies, waits for them, and re-layouts, refine(): jnp.broadcast_to(values[:, None, :, None, :, None], (rows, 2, cols, 2, de...  25.4 us
    ppermute x18, starting transfers between devices, with_halo(): after = lax.ppermute(initial, axis, down)  23.4 us
  transfers between devices with their start and end apart: 38, of which 15 were waited for; matrix products, arithmetic and copies ran while one was open for 44% of the time, Pallas kernels for 0%

commit v1 on v0

v1 whole, which is shorter than its diff:
```python
import functools
import math

import jax
import jax.numpy as jnp
import numpy as np
from jax import lax
from jax.experimental import pallas as pl
from jax.experimental.pallas import tpu as pltpu
from jax.sharding import PartitionSpec as P

NPTS = 1024
SWEEPS_LOW = 8
RELAX = 0.8
MESH = pl.DeviceIdType.MESH
HIGHEST = lax.Precision.HIGHEST
GROUPS = 4


def exact_dot(a, b):
    return jnp.dot(a, b, precision=HIGHEST, preferred_element_type=jnp.float32)


def flag_dot(a, b):
    return jnp.dot(
        a.astype(jnp.bfloat16), b.astype(jnp.bfloat16), preferred_element_type=jnp.float32
    )


def iota(shape, dim):
    return lax.broadcasted_iota(jnp.int32, shape, dim)


def ones_where(condition):
    return jnp.where(condition, 1.0, 0.0).astype(jnp.float32)


def ahead(value, axis):
    return pltpu.roll(value, value.shape[axis] - 1, axis)


def behind(value, axis):
    return pltpu.roll(value, 1, axis)


def sides(shape, width):
    nd = len(shape)
    row = iota(shape, nd - 2)
    col = iota(shape, nd - 1) & (width - 1)
    last_row = row == shape[-2] - 1
    last_col = col == width - 1
    extra = ones_where(row == 0) + ones_where(last_row)
    extra = extra + ones_where(col == 0) + ones_where(last_col)
    return last_row, last_col, extra


def plane_faces(center, edges):
    last_row, last_col, extra = edges
    nd = center.ndim
    north = jnp.where(last_row, 0.0, 0.5 * (center + ahead(center, nd - 2)))
    above = jnp.where(last_col, 0.0, 0.5 * (center + ahead(center, nd - 1)))
    total = north + behind(north, nd - 2) + above + behind(above, nd - 1)
    return north, above, total + center * extra


def plane_sum(field, north, above):
    nd = field.ndim
    total = north * ahead(field, nd - 2) + behind(north * field, nd - 2)
    return total + above * ahead(field, nd - 1) + behind(above * field, nd - 1)


def packed_ahead(wide, width):
    upper, lower = wide[1:], wide[:-1]
    lane = iota(upper.shape, 2)
    return pltpu.roll(jnp.where(lane < width, upper, lower), 128 - width, 2)


def packed_behind(wide, width):
    upper, lower = wide[1:], wide[:-1]
    lane = iota(upper.shape, 2)
    return pltpu.roll(jnp.where(lane >= 128 - width, lower, upper), width, 2)


def packed_faces(wide, width):
    center = wide[1:-1]
    east = 0.5 * (center + packed_ahead(wide, width)[1:])
    west = 0.5 * (center + packed_behind(wide, width)[:-1])
    north, above, total = plane_faces(center, sides(center.shape, width))
    return east, west, north, above, total + east + west


def packed_sum(wide, width, east, west, north, above):
    total = east * packed_ahead(wide, width)[1:] + west * packed_behind(wide, width)[:-1]
    return total + plane_sum(wide[1:-1], north, above)


def kernel(
    spaces,
    shifts,
    residual,
    log_base,
    mask,
    generator,
    point,
    offset,
    table_x,
    table_y,
    table_z,
    amplitude,
    correction,
    mean_field,
    square_field,
    cond,
    rhs,
    face_x,
    face_y,
    face_z,
    diag,
    gain,
    field_a,
    field_b,
    top_halo,
    flags,
    pairs,
    cond_mid,
    rhs_mid,
    mid_halo,
    faces_mid,
    field_mid,
    grown_mid,
    cond_low,
    rhs_low,
    faces_low,
    field_low,
    grown_low,
    arrived,
    copy_sem,
    halo_send,
    halo_recv,
    slab_send,
    slab_recv,
    sum_send,
    sum_recv,
):
    shift = lax.axis_index("shift")
    place = lax.axis_index("space")
    planes, width = log_base.shape[0], log_base.shape[1]
    blocks = mask.shape[0]
    has_left = place > 0
    has_right = place < spaces - 1
    rows = width // shifts

    barrier = pltpu.get_barrier_semaphore()
    near = [(d, place >= d, place < spaces - d) for d in range(1, 4)]
    for d, lower, upper in near:

        @pl.when(lower)
        def _():
            pl.semaphore_signal(barrier, inc=1, device_id={"space": place - d}, device_id_type=MESH)

        @pl.when(upper)
        def _():
            pl.semaphore_signal(barrier, inc=1, device_id={"space": place + d}, device_id_type=MESH)

    for d in range(1, shifts):
        pl.semaphore_signal(
            barrier, inc=1, device_id={"shift": (shift + d) % shifts}, device_id_type=MESH
        )
    own_rhs = pltpu.make_async_copy(residual.at[0], rhs.at[pl.ds(2, planes)], copy_sem)
    own_rhs.start()
    peers = shifts - 1
    for d in range(1, 4):
        peers = peers + (place + spaces - d) // spaces + (2 * spaces - 1 - place - d) // spaces
    pl.semaphore_wait(barrier, peers)

    def exchange(kind, to_left, left_lands, to_right, right_lands):
        leftward = pltpu.make_async_remote_copy(
            src_ref=to_left,
            dst_ref=left_lands,
            send_sem=halo_send.at[kind, 0],
            recv_sem=halo_recv.at[kind, 0],
            device_id={"space": place - 1},
            device_id_type=MESH,
        )
        rightward = pltpu.make_async_remote_copy(
            src_ref=to_right,
            dst_ref=right_lands,
            send_sem=halo_send.at[kind, 1],
            recv_sem=halo_recv.at[kind, 1],
            device_id={"space": place + 1},
            device_id_type=MESH,
        )

        def start():
            pl.when(has_left)(leftward.start)
            pl.when(has_right)(rightward.start)

        def arrive():
            pl.when(has_right)(leftward.wait_recv)
            pl.when(has_left)(rightward.wait_recv)

        def sent():
            pl.when(has_left)(leftward.wait_send)
            pl.when(has_right)(rightward.wait_send)

        return start, arrive, sent

    def spread(kind, slabs):
        made = []
        for d, lower, upper in near:
            leftward = pltpu.make_async_remote_copy(
                src_ref=slabs.at[3],
                dst_ref=slabs.at[3 + d],
                send_sem=slab_send.at[kind, 0, d - 1],
                recv_sem=slab_recv.at[kind, 0, d - 1],
                device_id={"space": place - d},
                device_id_type=MESH,
            )
            rightward = pltpu.make_async_remote_copy(
                src_ref=slabs.at[3],
                dst_ref=slabs.at[3 - d],
                send_sem=slab_send.at[kind, 1, d - 1],
                recv_sem=slab_recv.at[kind, 1, d - 1],
                device_id={"space": place + d},
                device_id_type=MESH,
            )
            made.append((lower, upper, leftward, rightward))

        def start():
            for lower, upper, leftward, rightward in made:
                pl.when(lower)(leftward.start)
                pl.when(upper)(rightward.start)

        def arrive():
            for lower, upper, leftward, rightward in made:
                pl.when(upper)(leftward.wait_recv)
                pl.when(lower)(rightward.wait_recv)

        def sent():
            for lower, upper, leftward, rightward in made:
                pl.when(lower)(leftward.wait_send)
                pl.when(upper)(rightward.wait_send)

        return start, arrive, sent

    end = planes + 2
    rhs_copy = exchange(
        0,
        residual.at[0, pl.ds(0, 2)],
        rhs.at[pl.ds(end, 2)],
        residual.at[0, pl.ds(planes - 2, 2)],
        rhs.at[pl.ds(0, 2)],
    )
    cond_copy = exchange(
        1,
        cond.at[pl.ds(3, 3)],
        cond.at[pl.ds(planes + 3, 3)],
        cond.at[pl.ds(planes, 3)],
        cond.at[pl.ds(0, 3)],
    )
    top_copy = exchange(
        2,
        field_b.at[pl.ds(2, 2)],
        top_halo.at[pl.ds(2, 2)],
        field_b.at[pl.ds(planes, 2)],
        top_halo.at[pl.ds(0, 2)],
    )
    cond_mid_copy = exchange(
        3,
        cond_mid.at[pl.ds(2, 2)],
        cond_mid.at[pl.ds(6, 2)],
        cond_mid.at[pl.ds(4, 2)],
        cond_mid.at[pl.ds(0, 2)],
    )
    rhs_mid_copy = exchange(
        4, rhs_mid.at[1], rhs_mid.at[5], rhs_mid.at[4], rhs_mid.at[0]
    )
    mid_copy = exchange(
        5,
        field_mid.at[pl.ds(1, 2)],
        mid_halo.at[pl.ds(2, 2)],
        field_mid.at[pl.ds(3, 2)],
        mid_halo.at[pl.ds(0, 2)],
    )
    cond_low_copy = spread(0, cond_low)
    rhs_low_copy = spread(1, rhs_low)

    rhs_copy[0]()

    lattice = (point[0] * generator[...]) & (NPTS - 1)
    shifted = lattice.astype(jnp.float32) / NPTS + offset[...]
    fraction = shifted - jnp.floor(shifted)
    weights = amplitude[...] * (1.0 - 2.0 * jnp.abs(2.0 * fraction - 1.0))

    def conductivity(i):
        along = weights * table_x[pl.ds(place * planes + i, 1), :]
        smooth = exact_dot(table_y[...] * along, table_z[...])
        cond[i + 3] = jnp.exp(log_base[i].astype(jnp.float32) + smooth)

    @pl.loop(0, 3)
    def _(i):
        conductivity(i)
        conductivity(planes - 3 + i)

    cond_copy[0]()

    @pl.loop(0, (planes - 6) // 2)
    def _(i):
        conductivity(3 + 2 * i)
        conductivity(4 + 2 * i)

    half = iota((2 * width, 128), 0)
    lane = iota((2 * width, 128), 1)
    gather_mid = ones_where(lane == 64 * (half // 128) + (half & 127) // 2)
    part = iota((4 * 128, 128), 0)
    lane = iota((4 * 128, 128), 1)
    gather_low = ones_where(lane == 32 * (part // 128) + (part & 63) // 2)

    def to_mid(scale):
        folded = []
        for k in range(4):
            pair = [
                pairs[2 * k + h, pl.ds(0, 64, 2), :] + pairs[2 * k + h, pl.ds(1, 64, 2), :]
                for h in range(2)
            ]
            folded.append(jnp.concatenate(pair, axis=1))
        made = scale * exact_dot(jnp.concatenate(folded, axis=0), gather_mid)
        return made.reshape(4, 64, 128)

    def to_low(scale, source, first):
        folded = [
            source[first + q, pl.ds(0, 32, 2), :] + source[first + q, pl.ds(1, 32, 2), :]
            for q in range(4)
        ]
        return scale * exact_dot(jnp.concatenate(folded, axis=1), gather_low)

    @pl.loop(0, planes // 2)
    def _(i):
        pairs[i] = cond[3 + 2 * i] + cond[4 + 2 * i]

    cond_mid[pl.ds(2, 4)] = to_mid(0.125)
    cond_mid_copy[0]()
    cond_low[3] = to_low(0.125, cond_mid, 2)
    cond_low_copy[0]()

    def block(number):
        inside = jnp.where((number >= 0) & (number < blocks), 1.0, 0.0)
        return mask[(number + blocks) % blocks].astype(jnp.float32) * inside

    cols = mask.shape[1]
    up_top = ones_where(iota((width, cols), 0) // 8 == iota((width, cols), 1))
    out_top = ones_where(iota((cols, 128), 1) // 8 == iota((cols, 128), 0))
    up_mid = ones_where(iota((64, cols), 0) // 4 == iota((64, cols), 1))
    out_mid = ones_where((iota((cols, 128), 1) & 63) // 4 == iota((cols, 128), 0))
    up_low = ones_where(iota((32, cols), 0) // 2 == iota((32, cols), 1))
    col = iota((cols, 128), 1)
    out_low = [
        ones_where(((col & 31) // 2 == iota((cols, 128), 0)) & (col // 64 == h)) for h in range(2)
    ]
    active_mid = []
    for k in range(4):
        one = block(2 * place + k - 1)
        flags[k] = flag_dot(flag_dot(up_top, one), out_top)
        active_mid.append(flag_dot(flag_dot(up_mid, one), out_mid))
    active_mid = jnp.stack([active_mid[j] for j in (0, 1, 1, 2, 2, 3)])
    active_low = []
    for s in range(-3, 4):
        parts = [flag_dot(block(2 * (place + s) + h), out_low[h]) for h in range(2)]
        active_low.append(flag_dot(up_low, parts[0] + parts[1]))
    active_low = jnp.stack(active_low)

    own_rhs.wait()
    rhs_copy[1]()
    cond_copy[1]()

    @pl.when(place == 0)
    def _():
        for i in range(3):
            cond[i] = cond[3]
        rhs[pl.ds(0, 2)] = jnp.zeros((2, width, 128), jnp.float32)

    @pl.when(place == spaces - 1)
    def _():
        for i in range(3):
            cond[planes + 3 + i] = cond[planes + 2]
        rhs[pl.ds(end, 2)] = jnp.zeros((2, width, 128), jnp.float32)

    edges = sides((width, 128), 128)

    @pl.loop(0, planes + 4)
    def _(i):
        center = cond[i + 1]
        west = 0.5 * (cond[i] + center)
        east = 0.5 * (center + cond[i + 2])
        north, above, total = plane_faces(center, edges)
        total = total + west + east
        face_x[i] = west
        face_x[i + 1] = east
        face_y[i] = north
        face_z[i] = above
        diag[i] = total
        scale = RELAX * flags[(i + 6) // 8] / total
        gain[i] = scale
        field_a[i] = scale * rhs[i]

    def around(source, i):
        total = face_x[i] * source[i - 1] + face_x[i + 1] * source[i + 1]
        return rhs[i] + total + plane_sum(source[i], face_y[i], face_z[i])

    def swept(source, i):
        kept = (1.0 - RELAX) * flags[(i + 6) // 8] * source[i]
        return kept + gain[i] * around(source, i)

    @pl.loop(1, planes + 3)
    def _(i):
        field_b[i] = swept(field_a, i)

    top_copy[0]()

    def left_over(i):
        return flags[(i + 6) // 8] * (around(field_b, i) - diag[i] * field_b[i])

    @pl.loop(0, planes // 2)
    def _(i):
        pairs[i] = left_over(2 + 2 * i) + left_over(3 + 2 * i)

    rhs_mid[pl.ds(1, 4)] = to_mid(0.5)
    rhs_mid_copy[0]()

    cond_mid_copy[1]()

    @pl.when(place == 0)
    def _():
        outer = pltpu.roll(cond_mid[2], 64, 1)
        cond_mid[0] = outer
        cond_mid[1] = outer

    @pl.when(place == spaces - 1)
    def _():
        outer = pltpu.roll(cond_mid[5], 64, 1)
        cond_mid[6] = outer
        cond_mid[7] = outer

    east, west, north, above, total = packed_faces(cond_mid[...], 64)
    faces_mid[0] = east
    faces_mid[1] = west
    faces_mid[2] = north
    faces_mid[3] = above
    faces_mid[4] = total
    faces_mid[5] = RELAX * active_mid / total
    faces_mid[6] = active_mid

    rhs_mid_copy[1]()

    @pl.when(place == 0)
    def _():
        rhs_mid[0] = jnp.zeros((64, 128), jnp.float32)

    @pl.when(place == spaces - 1)
    def _():
        rhs_mid[5] = jnp.zeros((64, 128), jnp.float32)

    nothing_mid = jnp.zeros((1, 64, 128), jnp.float32)

    def around_mid(wide):
        return rhs_mid[...] + packed_sum(
            wide, 64, faces_mid[0], faces_mid[1], faces_mid[2], faces_mid[3]
        )

    def swept_mid(wide):
        kept = (1.0 - RELAX) * faces_mid[6] * wide[1:-1]
        return kept + faces_mid[5] * around_mid(wide)

    def widened_mid(value):
        return jnp.concatenate([nothing_mid, value, nothing_mid], axis=0)

    solved_mid = swept_mid(widened_mid(faces_mid[5] * rhs_mid[...]))
    field_mid[...] = solved_mid
    mid_copy[0]()
    rest = faces_mid[6] * (around_mid(widened_mid(solved_mid)) - faces_mid[4] * solved_mid)
    grown_mid[pl.ds(0, 6)] = rest
    rhs_low[3] = to_low(0.5, grown_mid, 1)
    rhs_low_copy[0]()

    cond_low_copy[1]()
    for s in (1, 2, 3):

        @pl.when(place < s)
        def _():
            cond_low[3 - s] = pltpu.roll(cond_low[4 - s], 96, 1)

        @pl.when(place >= spaces - s)
        def _():
            cond_low[3 + s] = pltpu.roll(cond_low[2 + s], 32, 1)

    wide = cond_low[...]
    wide = jnp.concatenate([wide[:1], wide, wide[-1:]], axis=0)
    east, west, north, above, total = packed_faces(wide, 32)
    faces_low[0] = east
    faces_low[1] = west
    faces_low[2] = north
    faces_low[3] = above
    faces_low[4] = RELAX * active_low / total
    faces_low[5] = (1.0 - RELAX) * active_low

    rhs_low_copy[1]()
    for s in (1, 2, 3):

        @pl.when(place < s)
        def _():
            rhs_low[3 - s] = jnp.zeros((32, 128), jnp.float32)

        @pl.when(place >= spaces - s)
        def _():
            rhs_low[3 + s] = jnp.zeros((32, 128), jnp.float32)

    nothing_low = jnp.zeros((1, 32, 128), jnp.float32)
    field_low[...] = faces_low[4] * rhs_low[...]

    @pl.loop(0, SWEEPS_LOW - 1)
    def _(step):
        value = field_low[...]
        wide = jnp.concatenate([nothing_low, value, nothing_low], axis=0)
        total = rhs_low[...] + packed_sum(
            wide, 32, faces_low[0], faces_low[1], faces_low[2], faces_low[3]
        )
        field_low[...] = faces_low[5] * value + faces_low[4] * total

    repeat_low = jnp.where(
        iota((128, 4 * 128), 0)
        == 32 * (iota((128, 4 * 128), 1) // 128) + (iota((128, 4 * 128), 1) & 63) // 2,
        1.0,
        0.0,
    ).astype(jnp.float32)
    grown = exact_dot(field_low[pl.ds(2, 3)].reshape(3 * 32, 128), repeat_low)
    for k in range(-2, 6):
        s, q = (k + 4) // 4, (k + 4) % 4
        piece = grown[32 * s : 32 * s + 32, 128 * q : 128 * q + 128]
        grown_mid[k + 2, pl.ds(0, 32, 2), :] = piece
        grown_mid[k + 2, pl.ds(1, 32, 2), :] = piece

    mid_copy[1]()

    @pl.when(place == 0)
    def _():
        mid_halo[pl.ds(0, 2)] = jnp.zeros((2, 64, 128), jnp.float32)

    @pl.when(place == spaces - 1)
    def _():
        mid_halo[pl.ds(2, 2)] = jnp.zeros((2, 64, 128), jnp.float32)

    wide = grown_mid[...] + jnp.concatenate(
        [mid_halo[pl.ds(0, 2)], field_mid[pl.ds(1, 4)], mid_halo[pl.ds(2, 2)]], axis=0
    )
    solved_mid = swept_mid(widened_mid(swept_mid(wide)))

    repeat_mid = jnp.where(
        iota((128, 256), 0) == 64 * (iota((128, 256), 1) // 128) + (iota((128, 256), 1) & 127) // 2,
        1.0,
        0.0,
    ).astype(jnp.float32)
    grown = exact_dot(solved_mid.reshape(6 * 64, 128), repeat_mid)
    for m in range(-1, planes // 2 + 1):
        k, h = (m + 2) // 2, (m + 2) % 2
        piece = grown[64 * k : 64 * k + 64, 128 * h : 128 * h + 128]
        grown_low[m + 1, pl.ds(0, 64, 2), :] = piece
        grown_low[m + 1, pl.ds(1, 64, 2), :] = piece

    top_copy[1]()

    @pl.when(place == 0)
    def _():
        top_halo[pl.ds(0, 2)] = jnp.zeros((2, width, 128), jnp.float32)

    @pl.when(place == spaces - 1)
    def _():
        top_halo[pl.ds(2, 2)] = jnp.zeros((2, width, 128), jnp.float32)

    for i in range(2):
        field_a[i] = top_halo[i] + grown_low[0]
        field_a[end + i] = top_halo[2 + i] + grown_low[planes // 2 + 1]

    @pl.loop(0, planes // 2)
    def _(i):
        piece = grown_low[i + 1]
        field_a[2 + 2 * i] = field_b[2 + 2 * i] + piece
        field_a[3 + 2 * i] = field_b[3 + 2 * i] + piece

    top_copy[2]()

    @pl.loop(1, planes + 3)
    def _(i):
        field_b[i] = swept(field_a, i)

    chunk = planes // GROUPS
    sends = []
    for g in range(GROUPS):

        @pl.loop(0, chunk)
        def _(i):
            correction[0, g * chunk + i] = swept(field_b, g * chunk + i + 2)

        for d in range(1, shifts):
            peer = (shift + d) % shifts
            copy = pltpu.make_async_remote_copy(
                src_ref=correction.at[
                    0, pl.ds(g * chunk, chunk), pl.ds(pl.multiple_of(peer * rows, 8), rows), :
                ],
                dst_ref=arrived.at[d - 1, pl.ds(g * chunk, chunk)],
                send_sem=sum_send.at[d - 1, g],
                recv_sem=sum_recv.at[d - 1, g],
                device_id={"shift": peer},
                device_id_type=MESH,
            )
            copy.start()
            sends.append(copy)

    own_rows = pl.ds(pl.multiple_of(shift * rows, 8), rows)
    for g in range(GROUPS):
        span = pl.ds(g * chunk, chunk)
        value = correction[0, span, own_rows, :]
        total, squares = value, value * value
        for d in range(1, shifts):
            sends[g * (shifts - 1) + d - 1].wait_recv()
            value = arrived[d - 1, span]
            total = total + value
            squares = squares + value * value
        mean_field[span] = total / shifts
        square_field[span] = squares / shifts
    for copy in sends:
        copy.wait_send()
    for group in (rhs_copy, cond_copy, cond_mid_copy, rhs_mid_copy, mid_copy):
        group[2]()
    cond_low_copy[2]()
    rhs_low_copy[2]()


def mode_tables(modes):
    order = np.arange(modes)
    along_x = (order % 4 + 1).astype(np.float64)
    along_y = (order // 4 % 4 + 1).astype(np.float64)
    along_z = (order // 16 + 1).astype(np.float64)
    amplitude = 1.5 / np.sqrt(along_x * along_x + along_y * along_y + along_z * along_z)
    return along_x, along_y, along_z, amplitude


def cosines(frequency, cells):
    position = np.arange(cells) + 0.5
    return np.cos(math.pi * frequency[None, :] * position[:, None] / cells).astype(np.float32)


def local(spaces, shifts, residual, log_base, mask, gen_vector, point_index, shift_values):
    planes, width, depth = log_base.shape
    modes = gen_vector.shape[0]
    along_x, along_y, along_z, amplitude = mode_tables(modes)
    table_x = jnp.asarray(cosines(along_x, planes * spaces))
    table_y = jnp.asarray(cosines(along_y, width))
    table_z = jnp.asarray(np.ascontiguousarray(cosines(along_z, depth).T))
    amplitude = jnp.asarray(amplitude.astype(np.float32)[None])
    rows = width // shifts
    f32 = jnp.float32
    vmem = pl.BlockSpec(memory_space=pltpu.VMEM)

    def top(count):
        return pltpu.VMEM((count, width, depth), f32)

    return pl.pallas_call(
        functools.partial(kernel, spaces, shifts),
        out_shape=(
            jax.ShapeDtypeStruct((1, planes, width, depth), f32),
            jax.ShapeDtypeStruct((planes, rows, depth), f32),
            jax.ShapeDtypeStruct((planes, rows, depth), f32),
        ),
        in_specs=[
            pl.BlockSpec(memory_space=pl.ANY),
            vmem,
            vmem,
            vmem,
            pl.BlockSpec(memory_space=pltpu.SMEM),
            vmem,
            vmem,
            vmem,
            vmem,
            vmem,
        ],
        out_specs=(vmem, vmem, vmem),
        scratch_shapes=[
            top(planes + 6),
            top(planes + 4),
            top(planes + 5),
            top(planes + 4),
            top(planes + 4),
            top(planes + 4),
            top(planes + 4),
            top(planes + 4),
            top(planes + 4),
            top(4),
            top(4),
            top(planes // 2),
            pltpu.VMEM((8, 64, 128), f32),
            pltpu.VMEM((6, 64, 128), f32),
            pltpu.VMEM((4, 64, 128), f32),
            pltpu.VMEM((7, 6, 64, 128), f32),
            pltpu.VMEM((6, 64, 128), f32),
            pltpu.VMEM((8, 64, 128), f32),
            pltpu.VMEM((7, 32, 128), f32),
            pltpu.VMEM((7, 32, 128), f32),
            pltpu.VMEM((6, 7, 32, 128), f32),
            pltpu.VMEM((7, 32, 128), f32),
            top(planes // 2 + 2),
            pltpu.VMEM((shifts - 1, planes, rows, depth), f32),
            pltpu.SemaphoreType.DMA,
            pltpu.SemaphoreType.DMA((6, 2)),
            pltpu.SemaphoreType.DMA((6, 2)),
            pltpu.SemaphoreType.DMA((2, 2, 3)),
            pltpu.SemaphoreType.DMA((2, 2, 3)),
            pltpu.SemaphoreType.DMA((shifts - 1, GROUPS)),
            pltpu.SemaphoreType.DMA((shifts - 1, GROUPS)),
        ],
        compiler_params=pltpu.CompilerParams(
            collective_id=0, has_side_effects=True, vmem_limit_bytes=48 * 1024 * 1024
        ),
        name="cycle",
    )(
        residual,
        log_base,
        mask,
        gen_vector[None],
        point_index,
        shift_values,
        table_x,
        table_y,
        table_z,
        amplitude,
    )


def solution(mesh):
    placed = (
        P("shift", "space", None, None),
        P("space", None, None),
        P(),
        P(),
        P("shift"),
        P("shift", None),
    )
    return jax.shard_map(
        functools.partial(local, mesh.shape["space"], mesh.shape["shift"]),
        mesh=mesh,
        in_specs=placed,
        out_specs=(
            P("shift", "space", None, None),
            P("space", "shift", None),
            P("space", "shift", None),
        ),
        check_vma=False,
    )
```

time: 563 us -> 53.4 us (0.09)
  local copies, waits for them, and re-layouts: 276 us -> 8.64 us
  starting transfers between devices: 96.4 us -> 0 us
  other arithmetic: 87 us -> 0 us
  waiting for transfers between devices: 81.6 us -> 0 us
  Pallas kernels: 0 us -> 43 us
  between operations: 15.9 us -> 1.32 us
    reshape x8 -> x0, local copies, waits for them, and re-layouts: 223 us -> none  [the longest x3 148 us: coarsen(): values.reshape(rows // 2, 2, cols // 2, 2, depth // 2, 2)]
    ppermute x36 -> x0, starting transfers between devices: 96.3 us -> none  [the longest x18 72.9 us: with_halo(): before = lax.ppermute(last, axis, up)]
    reduce_scatter x2 -> x0, waiting for transfers between devices: 59.3 us -> none  [the longest x1 29.8 us: local(): lax.psum_scatter(solution_top, 'shift', scatter_dimension=1, tiled=True)]
    reduce_sum x4 -> x0, other arithmetic: 50.4 us -> none  [coarsen(): values.reshape(rows // 2, 2, cols // 2, 2, depth // 2, 2)]
    pallas_call x0 -> x1, Pallas kernels: none -> 43 us  [local(): pl.pallas_call(functools.partial(kernel, spaces, shifts), out_shape=(jax....]
    broadcast_in_dim x5 -> x0, local copies, waits for them, and re-layouts: 36.3 us -> none  [the longest x2 25.4 us: refine(): jnp.broadcast_to(values[:, None, :, None, :, None], (rows, 2, cols, 2, de...]
    mul x25 -> x0, other arithmetic: 25.7 us -> none  [the longest x12 10.8 us: more_sweeps(): solution = active * (solution + RELAX * (source - applied) / faces[6])]
    ppermute x36 -> x0, waiting for transfers between devices: 21.6 us -> none  [the longest x18 21.6 us: with_halo(): after = lax.ppermute(initial, axis, down)]
  transfers between devices with their start and end apart: 38 -> 0, of which waited for: 15 -> 0; matrix products, arithmetic and copies ran while one was open for 44% -> 0% of each run, Pallas kernels for 0% -> 0%
where the time goes in v1:
time: 53.4 us; the launch traced here: 53 us
  Pallas kernels  43 us (81%)
  local copies, waits for them, and re-layouts  8.64 us (16%)
  between operations  1.32 us (2%)
    pallas_call x1, Pallas kernels, local(): pl.pallas_call(functools.partial(kernel, spaces, shifts), out_shape=(jax....  43 us
    unnamed x21, local copies, waits for them, and re-layouts  8.64 us

profile of v1, /device:TPU:0, one launch (start us, length us, event | category | flops | bytes accessed | tf_op | source)
XLA Modules:
  0.0 53.0 jit_solution(2872406038904819863)
XLA Ops:
  1.3 0.0 copy-start.6
  1.3 0.0 copy-start.7
  1.3 0.0 copy-start.8
  1.3 0.6 %copy-done.6 = s32[64]{0:T(128)S(1)} copy-done((s32[64]{0:T(128)S(1)}, s32[64]{0:T(128)}, u32[]{:S(2)}) %copy-start.6) | copy-done | bytes 280
  1.9 0.0 copy-done.7
  2.0 0.0 copy-done.8
  2.0 0.0 copy-start
  2.0 1.2 %copy-done = f32[1,16,128,128]{3,2,1,0:T(8,128)S(1)} copy-done((f32[1,16,128,128]{3,2,1,0:T(8,128)S(1)}, f32[1,16,128,128]{3,2,1,0:T(8,128)}, u32[]{:S(2)}) %copy-start) | copy-done | bytes 1048600
  3.2 0.0 copy-start.1
  3.2 1.0 %copy-done.1 = bf16[16,128,128]{2,1,0:T(8,128)(2,1)S(1)} copy-done((bf16[16,128,128]{2,1,0:T(8,128)(2,1)S(1)}, bf16[16,128,128]{2,1,0:T(8,128)(2,1)}, u32[]{:S(2)}) %copy-start.1) | copy-done | bytes 524312
  4.2 0.0 copy-start.2
  4.2 0.9 %copy-done.2 = s32[16,16,16]{2,1,0:T(8,128)S(1)} copy-done((s32[16,16,16]{2,1,0:T(8,128)S(1)}, s32[16,16,16]{2,1,0:T(8,128)}, u32[]{:S(2)}) %copy-start.2) | copy-done | bytes 16408
  5.1 0.0 copy-start.3
  5.1 0.8 %copy-done.3 = f32[128,64]{1,0:T(8,128)S(1)} copy-done((f32[128,64]{1,0:T(8,128)S(1)}, f32[128,64]{1,0:T(8,128)}, u32[]{:S(2)}) %copy-start.3) | copy-done | bytes 32792
  6.0 0.0 copy-start.4
  6.0 0.8 %copy-done.4 = f32[128,64]{1,0:T(8,128)S(1)} copy-done((f32[128,64]{1,0:T(8,128)S(1)}, f32[128,64]{1,0:T(8,128)}, u32[]{:S(2)}) %copy-start.4) | copy-done | bytes 32792
  6.8 0.0 copy-start.5
  6.8 0.8 %copy-done.5 = f32[64,128]{1,0:T(8,128)S(1)} copy-done((f32[64,128]{1,0:T(8,128)S(1)}, f32[64,128]{1,0:T(8,128)}, u32[]{:S(2)}) %copy-start.5) | copy-done | bytes 32792
  7.6 43.0 %cycle.1 = (f32[1,16,128,128]{3,2,1,0:T(8,128)S(1)}, f32[16,32,128]{2,1,0:T(8,128)S(1)}, f32[16,32,128]{2,1,0:T(8,128)S(1)}) custom-call(f32[1,16,128,128]{3,2,1,0:T(8,128)S(1)} %copy-done, bf16[16,128,128]{2,1,0:T(8,128)(2,1)S(1)} %copy-done.1, s32[16,16,16]{2,1,0:T(8,128)S(1)} %copy-done.2, s32[1,64]{1,0:T(1,128)S(1)} %bitcast.1, s32[1]{0:T(128)S(6)} %copy.16.point, ...), custom_call_target="tpu_custom_call" | custom-call | tf_op jit(solution)/shard_map/cycle/pallas_call | solution.py:667
  50.6 1.0 %copy.17 = f32[1,16,128,128]{3,2,1,0:T(8,128)} copy(f32[1,16,128,128]{3,2,1,0:T(8,128)S(1)} %get-tuple-element.6) | data formatting | bytes 2097152
  51.6 0.7 %copy.18 = f32[16,32,128]{2,1,0:T(8,128)} copy(f32[16,32,128]{2,1,0:T(8,128)S(1)} %get-tuple-element.7) | data formatting | bytes 524288
  52.3 0.7 %copy.19 = f32[16,32,128]{2,1,0:T(8,128)} copy(f32[16,32,128]{2,1,0:T(8,128)S(1)} %get-tuple-element.8) | data formatting | bytes 524288
Async XLA Ops:
  1.3 0.7 %copy-start.6 = (s32[64]{0:T(128)S(1)}, s32[64]{0:T(128)}, u32[]{:S(2)}) copy-start(s32[64]{0:T(128)} %param.13) | copy-start | bytes 772
  1.3 0.7 %copy-start.7 = (f32[1,64]{1,0:T(1,128)S(1)}, f32[1,64]{1,0:T(1,128)}, u32[]{:S(2)}) copy-start(f32[1,64]{1,0:T(1,128)} %offset.1) | copy-start | bytes 772
  1.3 0.7 %copy-start.8 = (f32[1,64]{1,0:T(1,128)S(1)}, f32[1,64]{1,0:T(1,128)}, u32[]{:S(2)}) copy-start(f32[1,64]{1,0:T(1,128)} %constant.11.clone.amplitude) | copy-start | bytes 772
  2.0 1.2 %copy-start = (f32[1,16,128,128]{3,2,1,0:T(8,128)S(1)}, f32[1,16,128,128]{3,2,1,0:T(8,128)}, u32[]{:S(2)}) copy-start(f32[1,16,128,128]{3,2,1,0:T(8,128)} %residual.1) | copy-start | bytes 3145732
  3.2 1.0 %copy-start.1 = (bf16[16,128,128]{2,1,0:T(8,128)(2,1)S(1)}, bf16[16,128,128]{2,1,0:T(8,128)(2,1)}, u32[]{:S(2)}) copy-start(bf16[16,128,128]{2,1,0:T(8,128)(2,1)} %log_base.1) | copy-start | bytes 1572868
  4.2 0.9 %copy-start.2 = (s32[16,16,16]{2,1,0:T(8,128)S(1)}, s32[16,16,16]{2,1,0:T(8,128)}, u32[]{:S(2)}) copy-start(s32[16,16,16]{2,1,0:T(8,128)} %mask.1) | copy-start | bytes 49156
  5.1 0.8 %copy-start.3 = (f32[128,64]{1,0:T(8,128)S(1)}, f32[128,64]{1,0:T(8,128)}, u32[]{:S(2)}) copy-start(f32[128,64]{1,0:T(8,128)} %constant.9.clone.table_y) | copy-start | bytes 98308
  6.0 0.8 %copy-start.4 = (f32[128,64]{1,0:T(8,128)S(1)}, f32[128,64]{1,0:T(8,128)}, u32[]{:S(2)}) copy-start(f32[128,64]{1,0:T(8,128)} %constant.8.clone.table_x) | copy-start | bytes 98308
  6.8 0.8 %copy-start.5 = (f32[64,128]{1,0:T(8,128)S(1)}, f32[64,128]{1,0:T(8,128)}, u32[]{:S(2)}) copy-start(f32[64,128]{1,0:T(8,128)} %constant.10.clone.table_z) | copy-start | bytes 98308

commit v2 on v1

--- a/solution.py
+++ b/solution.py
@@ -12,6 +12,7 @@
 NPTS = 1024
 SWEEPS_LOW = 8
 RELAX = 0.8
+HBM = pltpu.HBM
 MESH = pl.DeviceIdType.MESH
 HIGHEST = lax.Precision.HIGHEST
 GROUPS = 4
@@ -98,15 +99,17 @@
     spaces,
     shifts,
     residual,
-    log_base,
-    mask,
-    generator,
-    point,
-    offset,
-    table_x,
-    table_y,
-    table_z,
-    amplitude,
+    *refs,
+):
+    sources, refs = refs[:9], refs[9:]
+    run(spaces, shifts, residual, sources, *refs)
+
+
+def run(
+    spaces,
+    shifts,
+    residual,
+    sources,
     correction,
     mean_field,
     square_field,
@@ -134,6 +137,15 @@
     field_low,
     grown_low,
     arrived,
+    log_base,
+    mask,
+    generator,
+    point,
+    offset,
+    table_x,
+    table_y,
+    table_z,
+    amplitude,
     copy_sem,
     halo_send,
     halo_recv,
@@ -150,6 +162,15 @@
     has_right = place < spaces - 1
     rows = width // shifts
 
+    held = (log_base, mask, generator, point, offset, table_x, table_y, table_z, amplitude)
+    fetches = [
+        pltpu.make_async_copy(source, target, copy_sem.at[n])
+        for n, (source, target) in enumerate(zip(sources, held))
+    ]
+    own_rhs = pltpu.make_async_copy(residual.at[0], rhs.at[pl.ds(2, planes)], copy_sem.at[9])
+    for fetch in fetches:
+        fetch.start()
+    own_rhs.start()
     barrier = pltpu.get_barrier_semaphore()
     near = [(d, place >= d, place < spaces - d) for d in range(1, 4)]
     for d, lower, upper in near:
@@ -166,8 +187,6 @@
         pl.semaphore_signal(
             barrier, inc=1, device_id={"shift": (shift + d) % shifts}, device_id_type=MESH
         )
-    own_rhs = pltpu.make_async_copy(residual.at[0], rhs.at[pl.ds(2, planes)], copy_sem)
-    own_rhs.start()
     peers = shifts - 1
     for d in range(1, 4):
         peers = peers + (place + spaces - d) // spaces + (2 * spaces - 1 - place - d) // spaces
@@ -286,8 +305,10 @@
     rhs_low_copy = spread(1, rhs_low)
 
     rhs_copy[0]()
-
-    lattice = (point[0] * generator[...]) & (NPTS - 1)
+    for fetch in fetches:
+        fetch.wait()
+
+    lattice = (point[...] * generator[...]) & (NPTS - 1)
     shifted = lattice.astype(jnp.float32) / NPTS + offset[...]
     fraction = shifted - jnp.floor(shifted)
     weights = amplitude[...] * (1.0 - 2.0 * jnp.abs(2.0 * fraction - 1.0))
@@ -370,25 +391,9 @@
     active_low = jnp.stack(active_low)
 
     own_rhs.wait()
-    rhs_copy[1]()
-    cond_copy[1]()
-
-    @pl.when(place == 0)
-    def _():
-        for i in range(3):
-            cond[i] = cond[3]
-        rhs[pl.ds(0, 2)] = jnp.zeros((2, width, 128), jnp.float32)
-
-    @pl.when(place == spaces - 1)
-    def _():
-        for i in range(3):
-            cond[planes + 3 + i] = cond[planes + 2]
-        rhs[pl.ds(end, 2)] = jnp.zeros((2, width, 128), jnp.float32)
-
     edges = sides((width, 128), 128)
 
-    @pl.loop(0, planes + 4)
-    def _(i):
+    def weigh(i):
         center = cond[i + 1]
         west = 0.5 * (cond[i] + center)
         east = 0.5 * (center + cond[i + 2])
@@ -411,9 +416,36 @@
         kept = (1.0 - RELAX) * flags[(i + 6) // 8] * source[i]
         return kept + gain[i] * around(source, i)
 
-    @pl.loop(1, planes + 3)
+    pl.loop(3, planes + 1, unroll=2)(weigh)
+
+    @pl.loop(4, planes, unroll=2)
     def _(i):
         field_b[i] = swept(field_a, i)
+
+    rhs_copy[1]()
+    cond_copy[1]()
+
+    @pl.when(place == 0)
+    def _():
+        for i in range(3):
+            cond[i] = cond[3]
+        rhs[pl.ds(0, 2)] = jnp.zeros((2, width, 128), jnp.float32)
+
+    @pl.when(place == spaces - 1)
+    def _():
+        for i in range(3):
+            cond[planes + 3 + i] = cond[planes + 2]
+        rhs[pl.ds(end, 2)] = jnp.zeros((2, width, 128), jnp.float32)
+
+    @pl.loop(0, 3)
+    def _(i):
+        weigh(i)
+        weigh(planes + 1 + i)
+
+    @pl.loop(0, 3)
+    def _(i):
+        field_b[1 + i] = swept(field_a, 1 + i)
+        field_b[planes + i] = swept(field_a, planes + i)
 
     top_copy[0]()
 
@@ -588,7 +620,7 @@
 
     top_copy[2]()
 
-    @pl.loop(1, planes + 3)
+    @pl.loop(1, planes + 3, unroll=2)
     def _(i):
         field_b[i] = swept(field_a, i)
 
@@ -596,7 +628,7 @@
     sends = []
     for g in range(GROUPS):
 
-        @pl.loop(0, chunk)
+        @pl.loop(0, chunk, unroll=2)
         def _(i):
             correction[0, g * chunk + i] = swept(field_b, g * chunk + i + 2)
 
@@ -664,6 +696,17 @@
     def top(count):
         return pltpu.VMEM((count, width, depth), f32)
 
+    small = (
+        log_base,
+        mask,
+        gen_vector[None],
+        point_index[None],
+        shift_values,
+        table_x,
+        table_y,
+        table_z,
+        amplitude,
+    )
     return pl.pallas_call(
         functools.partial(kernel, spaces, shifts),
         out_shape=(
@@ -671,18 +714,7 @@
             jax.ShapeDtypeStruct((planes, rows, depth), f32),
             jax.ShapeDtypeStruct((planes, rows, depth), f32),
         ),
-        in_specs=[
-            pl.BlockSpec(memory_space=pl.ANY),
-            vmem,
-            vmem,
-            vmem,
-            pl.BlockSpec(memory_space=pltpu.SMEM),
-            vmem,
-            vmem,
-            vmem,
-            vmem,
-            vmem,
-        ],
+        in_specs=[pl.BlockSpec(memory_space=HBM)] * (1 + len(small)),
         out_specs=(vmem, vmem, vmem),
         scratch_shapes=[
             top(planes + 6),
@@ -709,7 +741,8 @@
             pltpu.VMEM((7, 32, 128), f32),
             top(planes // 2 + 2),
             pltpu.VMEM((shifts - 1, planes, rows, depth), f32),
-            pltpu.SemaphoreType.DMA,
+            *[pltpu.VMEM(array.shape, array.dtype) for array in small],
+            pltpu.SemaphoreType.DMA((10,)),
             pltpu.SemaphoreType.DMA((6, 2)),
             pltpu.SemaphoreType.DMA((6, 2)),
             pltpu.SemaphoreType.DMA((2, 2, 3)),
@@ -718,20 +751,12 @@
             pltpu.SemaphoreType.DMA((shifts - 1, GROUPS)),
         ],
         compiler_params=pltpu.CompilerParams(
-            collective_id=0, has_side_effects=True, vmem_limit_bytes=48 * 1024 * 1024
+            collective_id=0, has_side_effects=True, vmem_limit_bytes=63 * 1024 * 1024
         ),
         name="cycle",
     )(
         residual,
-        log_base,
-        mask,
-        gen_vector[None],
-        point_index,
-        shift_values,
-        table_x,
-        table_y,
-        table_z,
-        amplitude,
+        *small,
     )
 
 

time: 53.4 us -> 46.8 us (0.88)
  local copies, waits for them, and re-layouts: 8.64 us -> 4.09 us
  Pallas kernels: 43 us -> 41.3 us
    unnamed x21 -> x7, local copies, waits for them, and re-layouts: 8.64 us -> 4.09 us
    pallas_call x1, Pallas kernels: 43 us -> 41.3 us  [local(): pl.pallas_call(functools.partial(kernel, spaces, shifts), out_shape=(jax....]
where the time goes in v2:
time: 46.8 us; the launch traced here: 46.7 us
  Pallas kernels  41.3 us (88%)
  local copies, waits for them, and re-layouts  4.09 us (9%)
  between operations  1.3 us (3%)
    pallas_call x1, Pallas kernels, local(): pl.pallas_call(functools.partial(kernel, spaces, shifts), out_shape=(jax....  41.3 us
    unnamed x7, local copies, waits for them, and re-layouts  4.09 us

profile of v2, /device:TPU:0, one launch (start us, length us, event | category | flops | bytes accessed | tf_op | source)
XLA Modules:
  0.0 46.7 jit_solution(10978964234622806210)
XLA Ops:
  1.3 41.3 %cycle.1 = (f32[1,16,128,128]{3,2,1,0:T(8,128)}, f32[16,32,128]{2,1,0:T(8,128)}, f32[16,32,128]{2,1,0:T(8,128)}) custom-call(f32[1,16,128,128]{3,2,1,0:T(8,128)} %residual.1, bf16[16,128,128]{2,1,0:T(8,128)(2,1)} %refs_0_.1, s32[16,16,16]{2,1,0:T(8,128)} %refs_1_.1, s32[1,64]{1,0:T(1,128)} %bitcast.3, s32[1,1]{1,0:T(1,128)} %bitcast.2.refs_3_, ...), custom_call_target="tpu_custom_call" | custom-call | tf_op jit(solution)/shard_map/cycle/pallas_call | solution.py:710
  42.6 0.0 copy-start.1
  42.6 2.3 %copy.17 = f32[1,16,128,128]{3,2,1,0:T(8,128)} copy(f32[1,16,128,128]{3,2,1,0:T(8,128)} %get-tuple-element.6) | data formatting | bytes 2097152
  44.9 0.0 copy-done.1
  44.9 0.0 copy-start
  44.9 0.7 %copy.18 = f32[16,32,128]{2,1,0:T(8,128)} copy(f32[16,32,128]{2,1,0:T(8,128)S(1)} %copy-done.1) | data formatting | bytes 524288
  45.6 0.3 copy-done
  46.0 0.7 %copy.19 = f32[16,32,128]{2,1,0:T(8,128)} copy(f32[16,32,128]{2,1,0:T(8,128)S(1)} %copy-done) | data formatting | bytes 524288
Async XLA Ops:
  42.6 2.4 %copy-start.1 = (f32[16,32,128]{2,1,0:T(8,128)S(1)}, f32[16,32,128]{2,1,0:T(8,128)}, u32[]{:S(2)}) copy-start(f32[16,32,128]{2,1,0:T(8,128)} %get-tuple-element.7) | copy-start | bytes 786436
  44.9 1.0 %copy-start = (f32[16,32,128]{2,1,0:T(8,128)S(1)}, f32[16,32,128]{2,1,0:T(8,128)}, u32[]{:S(2)}) copy-start(f32[16,32,128]{2,1,0:T(8,128)} %get-tuple-element.8) | copy-start | bytes 786436

commit v3 on v2

--- a/solution.py
+++ b/solution.py
@@ -15,7 +15,7 @@
 HBM = pltpu.HBM
 MESH = pl.DeviceIdType.MESH
 HIGHEST = lax.Precision.HIGHEST
-GROUPS = 4
+GROUPS = 8
 
 
 def exact_dot(a, b):
@@ -110,7 +110,7 @@
     shifts,
     residual,
     sources,
-    correction,
+    handed,
     mean_field,
     square_field,
     cond,
@@ -137,6 +137,7 @@
     field_low,
     grown_low,
     arrived,
+    correction,
     log_base,
     mask,
     generator,
@@ -620,13 +621,13 @@
 
     top_copy[2]()
 
-    @pl.loop(1, planes + 3, unroll=2)
-    def _(i):
-        field_b[i] = swept(field_a, i)
-
     chunk = planes // GROUPS
     sends = []
     for g in range(GROUPS):
+
+        @pl.loop(chunk * g + 3 if g else 1, chunk * g + chunk + 3, unroll=2)
+        def _(i):
+            field_b[i] = swept(field_a, i)
 
         @pl.loop(0, chunk, unroll=2)
         def _(i):
@@ -647,6 +648,8 @@
             copy.start()
             sends.append(copy)
 
+    own_copy = pltpu.make_async_copy(correction, handed, copy_sem.at[10])
+    own_copy.start()
     own_rows = pl.ds(pl.multiple_of(shift * rows, 8), rows)
     for g in range(GROUPS):
         span = pl.ds(g * chunk, chunk)
@@ -661,10 +664,25 @@
         square_field[span] = squares / shifts
     for copy in sends:
         copy.wait_send()
+    own_copy.wait()
     for group in (rhs_copy, cond_copy, cond_mid_copy, rhs_mid_copy, mid_copy):
         group[2]()
     cond_low_copy[2]()
     rhs_low_copy[2]()
+
+
+def hand_out(correction, mean_field, square_field, to_correction, to_mean, to_square, sem):
+    part = correction.shape[1] // 4
+    moves = [
+        (correction.at[0, pl.ds(k * part, part)], to_correction.at[0, pl.ds(k * part, part)])
+        for k in range(4)
+    ]
+    moves = moves + [(mean_field, to_mean), (square_field, to_square)]
+    copies = [pltpu.make_async_copy(*move, sem.at[n]) for n, move in enumerate(moves)]
+    for copy in copies:
+        copy.start()
+    for copy in copies:
+        copy.wait()
 
 
 def mode_tables(modes):
@@ -707,7 +725,7 @@
         table_z,
         amplitude,
     )
-    return pl.pallas_call(
+    results = pl.pallas_call(
         functools.partial(kernel, spaces, shifts),
         out_shape=(
             jax.ShapeDtypeStruct((1, planes, width, depth), f32),
@@ -715,7 +733,7 @@
             jax.ShapeDtypeStruct((planes, rows, depth), f32),
         ),
         in_specs=[pl.BlockSpec(memory_space=HBM)] * (1 + len(small)),
-        out_specs=(vmem, vmem, vmem),
+        out_specs=(pl.BlockSpec(memory_space=HBM), vmem, vmem),
         scratch_shapes=[
             top(planes + 6),
             top(planes + 4),
@@ -741,8 +759,9 @@
             pltpu.VMEM((7, 32, 128), f32),
             top(planes // 2 + 2),
             pltpu.VMEM((shifts - 1, planes, rows, depth), f32),
+            pltpu.VMEM((1, planes, width, depth), f32),
             *[pltpu.VMEM(array.shape, array.dtype) for array in small],
-            pltpu.SemaphoreType.DMA((10,)),
+            pltpu.SemaphoreType.DMA((11,)),
             pltpu.SemaphoreType.DMA((6, 2)),
             pltpu.SemaphoreType.DMA((6, 2)),
             pltpu.SemaphoreType.DMA((2, 2, 3)),
@@ -758,6 +777,16 @@
         residual,
         *small,
     )
+    hbm = pl.BlockSpec(memory_space=HBM)
+    return pl.pallas_call(
+        hand_out,
+        out_shape=tuple(jax.ShapeDtypeStruct(part.shape, f32) for part in results),
+        in_specs=[hbm] * 3,
+        out_specs=(hbm,) * 3,
+        scratch_shapes=[pltpu.SemaphoreType.DMA((6,))],
+        compiler_params=pltpu.CompilerParams(vmem_limit_bytes=63 * 1024 * 1024),
+        name="hand_out",
+    )(*results)
 
 
 def solution(mesh):

time: 46.8 us -> 90.6 us (1.94)
  Pallas kernels: 41.3 us -> 89.2 us
  local copies, waits for them, and re-layouts: 4.09 us -> 0 us
    pallas_call x0 -> x1, Pallas kernels: none -> 48.8 us  [local(): pl.pallas_call(hand_out, out_shape=tuple((jax.ShapeDtypeStruct(part.shape...]
    unnamed x7 -> x0, local copies, waits for them, and re-layouts: 4.09 us -> none
    pallas_call x1, Pallas kernels: 41.3 us -> 40.4 us  [local(): pl.pallas_call(functools.partial(kernel, spaces, shifts), out_shape=(jax....]
where the time goes in v3:
time: 90.6 us; the launch traced here: 90.5 us
  Pallas kernels  89.2 us (98%)
  between operations  1.29 us (1%)
    pallas_call x1, Pallas kernels, local(): pl.pallas_call(hand_out, out_shape=tuple((jax.ShapeDtypeStruct(part.shape...  48.8 us
    pallas_call x1, Pallas kernels, local(): pl.pallas_call(functools.partial(kernel, spaces, shifts), out_shape=(jax....  40.4 us

profile of v3, /device:TPU:0, one launch (start us, length us, event | category | flops | bytes accessed | tf_op | source)
XLA Modules:
  0.0 90.5 jit_solution(1598328791167261445)
XLA Ops:
  1.3 40.4 %cycle.1 = (f32[1,16,128,128]{3,2,1,0:T(8,128)}, f32[16,32,128]{2,1,0:T(8,128)}, f32[16,32,128]{2,1,0:T(8,128)}) custom-call(f32[1,16,128,128]{3,2,1,0:T(8,128)} %residual.1, bf16[16,128,128]{2,1,0:T(8,128)(2,1)} %refs_0_.1, s32[16,16,16]{2,1,0:T(8,128)} %refs_1_.1, s32[1,64]{1,0:T(1,128)} %bitcast.3, s32[1,1]{1,0:T(1,128)} %bitcast.2.refs_3_, ...), custom_call_target="tpu_custom_call" | custom-call | tf_op jit(solution)/shard_map/cycle/pallas_call | solution.py:728
  41.7 48.8 %hand_out.1 = (f32[1,16,128,128]{3,2,1,0:T(8,128)}, f32[16,32,128]{2,1,0:T(8,128)}, f32[16,32,128]{2,1,0:T(8,128)}) custom-call(f32[1,16,128,128]{3,2,1,0:T(8,128)} %get-tuple-element.6.correction, f32[16,32,128]{2,1,0:T(8,128)} %get-tuple-element.7.mean_field, f32[16,32,128]{2,1,0:T(8,128)} %get-tuple-element.8.square_field), custom_call_target="tpu_custom_call" | custom-call | tf_op jit(solution)/shard_map/hand_out/pallas_call | solution.py:781

commit v4 on v3

--- a/solution.py
+++ b/solution.py
@@ -671,18 +671,28 @@
     rhs_low_copy[2]()
 
 
-def hand_out(correction, mean_field, square_field, to_correction, to_mean, to_square, sem):
+def hand_out(
+    correction, mean_field, square_field, to_correction, to_mean, to_square, *held_and_sems
+):
+    held_correction, held_mean, held_square, in_sem, out_sem = held_and_sems
     part = correction.shape[1] // 4
-    moves = [
-        (correction.at[0, pl.ds(k * part, part)], to_correction.at[0, pl.ds(k * part, part)])
-        for k in range(4)
-    ]
-    moves = moves + [(mean_field, to_mean), (square_field, to_square)]
-    copies = [pltpu.make_async_copy(*move, sem.at[n]) for n, move in enumerate(moves)]
-    for copy in copies:
-        copy.start()
-    for copy in copies:
-        copy.wait()
+    moves = []
+    for k in range(4):
+        span = pl.ds(k * part, part)
+        moves.append(
+            (correction.at[0, span], held_correction.at[0, span], to_correction.at[0, span])
+        )
+    moves.append((mean_field, held_mean, to_mean))
+    moves.append((square_field, held_square, to_square))
+    fetches = [pltpu.make_async_copy(m[0], m[1], in_sem.at[n]) for n, m in enumerate(moves)]
+    stores = [pltpu.make_async_copy(m[1], m[2], out_sem.at[n]) for n, m in enumerate(moves)]
+    for fetch in fetches:
+        fetch.start()
+    for fetch, store in zip(fetches, stores):
+        fetch.wait()
+        store.start()
+    for store in stores:
+        store.wait()
 
 
 def mode_tables(modes):
@@ -783,7 +793,11 @@
         out_shape=tuple(jax.ShapeDtypeStruct(part.shape, f32) for part in results),
         in_specs=[hbm] * 3,
         out_specs=(hbm,) * 3,
-        scratch_shapes=[pltpu.SemaphoreType.DMA((6,))],
+        scratch_shapes=[
+            *[pltpu.VMEM(part.shape, f32) for part in results],
+            pltpu.SemaphoreType.DMA((6,)),
+            pltpu.SemaphoreType.DMA((6,)),
+        ],
         compiler_params=pltpu.CompilerParams(vmem_limit_bytes=63 * 1024 * 1024),
         name="hand_out",
     )(*results)

time: 90.6 us -> 44 us (0.49)
  Pallas kernels: 89.2 us -> 42.6 us
    pallas_call x1, Pallas kernels: 48.8 us -> 2.19 us  [local(): pl.pallas_call(hand_out, out_shape=tuple((jax.ShapeDtypeStruct(part.shape...]
where the time goes in v4:
time: 44 us; the launch traced here: 43.8 us
  Pallas kernels  42.6 us (97%)
  between operations  1.29 us (3%)
    pallas_call x1, Pallas kernels, local(): pl.pallas_call(functools.partial(kernel, spaces, shifts), out_shape=(jax....  40.4 us
    pallas_call x1, Pallas kernels, local(): pl.pallas_call(hand_out, out_shape=tuple((jax.ShapeDtypeStruct(part.shape...  2.19 us

profile of v4, /device:TPU:0, one launch (start us, length us, event | category | flops | bytes accessed | tf_op | source)
XLA Modules:
  0.0 43.8 jit_solution(6129119676975333737)
XLA Ops:
  1.3 40.4 %cycle.1 = (f32[1,16,128,128]{3,2,1,0:T(8,128)}, f32[16,32,128]{2,1,0:T(8,128)}, f32[16,32,128]{2,1,0:T(8,128)}) custom-call(f32[1,16,128,128]{3,2,1,0:T(8,128)} %residual.1, bf16[16,128,128]{2,1,0:T(8,128)(2,1)} %refs_0_.1, s32[16,16,16]{2,1,0:T(8,128)} %refs_1_.1, s32[1,64]{1,0:T(1,128)} %bitcast.3, s32[1,1]{1,0:T(1,128)} %bitcast.2.refs_3_, ...), custom_call_target="tpu_custom_call" | custom-call | tf_op jit(solution)/shard_map/cycle/pallas_call | solution.py:738
  41.7 2.2 %hand_out.1 = (f32[1,16,128,128]{3,2,1,0:T(8,128)}, f32[16,32,128]{2,1,0:T(8,128)}, f32[16,32,128]{2,1,0:T(8,128)}) custom-call(f32[1,16,128,128]{3,2,1,0:T(8,128)} %get-tuple-element.6.correction, f32[16,32,128]{2,1,0:T(8,128)} %get-tuple-element.7.mean_field, f32[16,32,128]{2,1,0:T(8,128)} %get-tuple-element.8.square_field), custom_call_target="tpu_custom_call" | custom-call | tf_op jit(solution)/shard_map/hand_out/pallas_call | solution.py:791
